TPU v7x, 32 devices: a whole 2x2x4 slice. The times are simulated.
32 devices in a mesh: groups: 2 (over x), owner: 4 (over y, core), path: 4 (over z).
Axes of the slice: x: 2, y: 2, z: 4, core: 2. Of those that a mesh axis runs over, the one named last changes fastest.
Arguments:
- sensitivity: bfloat16 [32768, 2048], P(('groups', 'owner', 'path')), parts along dimension 0, may hold values from -0.03125 to 0.03125
- present_trade_value: float32 [32768], P(('groups', 'owner', 'path')), parts along dimension 0, may hold values from -2.5 to 2.5
- trade_set_owner: int32 [32768, 1], P(('groups', 'owner', 'path')), parts along dimension 0, may hold values from 0 to 3; in each aligned block of 1024 rows (0 to 1023, 1024 to 2047, ...) at most 1024 rows name the same one
- trade_local_set: int32 [32768], P(('groups', 'owner', 'path')), parts along dimension 0, may hold values from 0 to 255
- shocks: bfloat16 [256, 4, 2048], P(('groups', 'path')), parts along dimension 0, may hold values from -6 to 6
- collateral_of_set: int32 [2048], P(('groups', 'owner')), parts along dimension 0, may hold values from 0 to 31
- collateral_posted: float32 [64], P('groups'), parts along dimension 0, may hold values from 0.3 to 3
- discount: float32 [8], P('groups'), parts along dimension 0, may hold values from 0.5 to 1
Outputs:
- exposure_paths: float32 [2048, 512], P(('groups', 'owner'), 'path'), parts along dimension 0
- expected_exposure: float32 [2048, 4], P(('groups', 'owner')), parts along dimension 0
There are 2 independent parts, one for each index of `groups`. A program takes and returns all parts, laid end to end along the dimension named above; each array names one. Nothing has to cross between parts.
Inputs may be any that keep to these rules, and one draw needn't show every extreme that they name: `trade_set_owner`: within the trades of one device at most 1024 name one owner, a bound that some block reaches of them.
All inputs are finite; a program needn't handle non-finite values.
Results may differ from a plain program's by a relative error of at most 0.0035.
Values may be sent and summed in bfloat16 or wider, within the bound.
A program may use at most 64 MiB of HBM per device.

v0:
```python
import jax
import jax.numpy as jnp
from jax import lax
from jax.sharding import PartitionSpec as P


def shards(
    sensitivity,
    present_trade_value,
    trade_set_owner,
    trade_local_set,
    shocks,
    collateral_of_set,
    collateral_posted,
    discount,
):
    trade_count = sensitivity.shape[0]
    steps_count = shocks.shape[1]
    owners = lax.axis_size("owner")
    owner_local_sets = collateral_of_set.shape[0]
    shard_piece = lax.all_gather(shocks, "path", axis=0, tiled=True)
    path_count = shard_piece.shape[0]
    flat_shocks = shard_piece.reshape(path_count * steps_count, shard_piece.shape[2])
    product = lax.dot_general(
        sensitivity, flat_shocks, (((1,), (1,)), ((), ())), preferred_element_type=jnp.float32
    )
    trade_values = (product + present_trade_value[:, None]).astype(jnp.bfloat16)
    columns = trade_values.shape[1]
    owner_of = trade_set_owner[:, 0]
    capacity = 4 * trade_count // owners
    owner_hot = (owner_of[:, None] == jnp.arange(owners, dtype=jnp.int32)[None, :]).astype(
        jnp.int32
    )
    earlier = jnp.cumsum(owner_hot, axis=0) - owner_hot
    slot_index = jnp.sum(earlier * owner_hot, axis=1)
    outgoing = (
        jnp.zeros((owners, capacity, columns), jnp.bfloat16)
        .at[owner_of, slot_index]
        .set(trade_values)
    )
    out_labels = (
        jnp.full((owners, capacity), -1, jnp.int32).at[owner_of, slot_index].set(trade_local_set)
    )
    arrived, arrived_labels = (
        lax.all_to_all(outgoing, "owner", split_axis=0, concat_axis=0, tiled=True),
        lax.all_to_all(out_labels, "owner", split_axis=0, concat_axis=0, tiled=True),
    )
    set_hot = (
        jnp.arange(owner_local_sets, dtype=jnp.int32)[:, None] == arrived_labels.reshape(1, -1)
    ).astype(jnp.bfloat16)
    partial_nets = jnp.dot(
        set_hot, arrived.reshape(-1, columns), preferred_element_type=jnp.float32
    )
    net_values = lax.psum_scatter(partial_nets, "path", scatter_dimension=1, tiled=True)
    agreement_onehot = (
        collateral_of_set[:, None]
        == jnp.arange(collateral_posted.shape[0], dtype=jnp.int32)[None, :]
    ).astype(jnp.float32)
    floored_exposure = jnp.dot(
        agreement_onehot, collateral_posted[:, None], precision=lax.Precision.HIGHEST
    )
    local_paths = net_values.shape[1] // steps_count
    discounted = jnp.tile(discount, local_paths)[None, :] * jnp.maximum(
        net_values - floored_exposure, 0.0
    )
    local_totals = jnp.sum(discounted.reshape(owner_local_sets, local_paths, steps_count), axis=1)
    path_totals = lax.psum(local_totals, "path")
    expected = path_totals / (local_paths * lax.axis_size("path"))
    return (discounted, expected)


def solution(mesh):
    in_specs = (
        P(("groups", "owner", "path"), None),
        P(("groups", "owner", "path")),
        P(("groups", "owner", "path"), None),
        P(("groups", "owner", "path")),
        P(("groups", "path"), None, None),
        P(("groups", "owner")),
        P("groups"),
        P("groups"),
    )
    out_specs = (P(("groups", "owner"), "path"), P(("groups", "owner"), None))
    return jax.shard_map(shards, mesh=mesh, in_specs=in_specs, out_specs=out_specs, check_vma=False)
```

profile of v0, /device:TPU:0, one launch (start us, length us, event | category | flops | bytes accessed | tf_op | source)
XLA Modules:
  0.0 164.1 jit_solution(3408248479724428130)
XLA Ops:
  7.2 0.0 copy-start
  7.2 0.0 copy-start.3
  7.2 0.0 all-gather.2.cloned.1.call-start
  7.2 0.7 all-gather.2.cloned.1.call-update
  7.9 0.7 fusion.9
  8.6 1.1 reduce-window.6
  9.7 0.2 slice_reduce_fusion
  10.0 0.2 reduce-window.9
  10.1 0.1 add_bitcast_fusion
  10.2 0.7 fusion.8
  10.9 0.7 compare_select_fusion
  11.6 0.7 multiply_reduce_fusion
  12.4 0.8 and_reduce_fusion
  13.1 5.1 %scatter_custom_fusion = s32[4096]{0:T(1024)} fusion(s32[1024]{0:T(1024)S(1)} %broadcast_select_fusion, s32[1024]{0:T(1024)} %param.11, s32[]{:T(128)} %constant.7.clone.1), kind=kCustom, calls=%fused_computation.25 | custom fusion | bytes 16896
  18.2 4.2 %all-to-all-start = ((s32[4,1,1024]{2,1,0:T(1,128)}), s32[4,1,1024]{2,1,0:T(1,128)S(1)}, u32[]{:S(2)}, u32[]{:S(2)}) async-start(s32[4,1,1024]{2,1,0:T(1,128)} %bitcast.4), calls=%async_computation | async-start | bytes 32768 | tf_op jit(solution)/shard_map/all_to_all | solution.py:46
  22.4 0.0 reduce-scatter.2.cloned.1.call-start
  22.4 35.8 %all-gather.2.cloned.1.call-done = bf16[128,4,2048]{2,1,0:T(4,128)(2,1)} async-done(((bf16[32,4,2048]{2,1,0:T(4,128)(2,1)}), bf16[128,4,2048]{2,1,0:T(4,128)(2,1)}) %all-gather.2.cloned.1.call-update) | async-done | bytes 2097168 | tf_op jit(solution)/shard_map/all_gather | solution.py:21
  58.2 2.5 %reshape.56 = bf16[512,2048]{1,0:T(8,128)(2,1)S(1)} reshape(bf16[128,4,2048]{2,1,0:T(4,128)(2,1)} %all-gather.2.cloned.1.call-done) | data formatting | bytes 4194304 | tf_op jit(solution)/shard_map/reshape | solution.py:23
  60.8 0.0 copy-done.3
  60.8 4.6 %add_convert_fusion = bf16[1024,512]{1,0:T(8,128)(2,1)S(1)} fusion(bf16[1024,2048]{1,0:T(8,128)(2,1)} %param.8, bf16[512,2048]{1,0:T(8,128)(2,1)S(1)} %reshape.56, f32[1024]{0:T(1024)S(1)} %copy-done.3), kind=kOutput, calls=%fused_computation.6 | convolution fusion | flops 2148532224 | bytes 7344128 | tf_op jit(solution)/shard_map/dot_general | solution.py:24
  65.3 7.7 %scatter_custom_fusion.1 = bf16[4096,512]{1,0:T(8,128)(2,1)} fusion(s32[1024]{0:T(1024)S(1)} %broadcast_select_fusion, bf16[1024,512]{1,0:T(8,128)(2,1)S(1)} %add_convert_fusion, bf16[]{:T(256)} %constant.5.clone.1), kind=kCustom, calls=%fused_computation.4 | custom fusion | bytes 4194306
  73.1 0.0 all-to-all-done
  73.1 51.9 %all_to_all.14 = bf16[4,1024,512]{2,1,0:T(8,128)(2,1)S(1)} all-to-all(bf16[4,1024,512]{2,1,0:T(8,128)(2,1)} %bitcast.35), channel_id=1, replica_groups=mesh['groups'=2,'owner'=4,'path'=4] {'owner'}, dimensions={0} | all-to-all | bytes 8388608 | tf_op jit(solution)/shard_map/all_to_all | solution.py:45
  125.0 0.0 copy-start.2
  125.0 0.0 copy-start.4
  125.0 2.0 %fusion = f32[256,512]{1,0:T(8,128)} fusion(bf16[4096,512]{1,0:T(8,128)(2,1)S(1)} %bitcast.36, s32[4096]{0:T(1024)S(1)} %bitcast.39), kind=kOutput, calls=%fused_computation.3 | convolution fusion | flops 1074790400 | bytes 4734976 | tf_op jit(solution)/shard_map/dot_general | solution.py:51
  127.0 0.0 reduce-scatter.2.cloned.1.call-update
  127.1 0.0 copy-done.2
  127.1 0.1 mul.13
  127.2 0.0 copy-done
  127.2 0.0 copy-done.4
  127.2 0.2 fusion.4
  127.4 19.3 %reduce-scatter.2.cloned.1.call-done = f32[256,128]{1,0:T(8,128)} async-done(((f32[256,512]{1,0:T(8,128)}), f32[256,128]{1,0:T(8,128)}) %reduce-scatter.2.cloned.1.call-update) | async-done | bytes 131088 | tf_op jit(solution)/shard_map/reduce_scatter | solution.py:54
  146.7 1.0 maximum_multiply_fusion
  147.7 0.0 copy-start.1
  147.7 0.1 copy.11
  147.9 8.7 %psum.7 = f32[256,4]{0,1:T(4,128)S(1)} all-reduce(f32[256,4]{0,1:T(4,128)S(1)} %reduce_sum.22), channel_id=1, replica_groups=mesh['groups'=2,'owner'=4,'path'=4] {'path'}, use_global_device_ids=true, to_apply=%region_7.8 | all-reduce | flops 1024 | bytes 8192 | tf_op jit(solution)/shard_map/psum | solution.py:67
  156.7 0.6 broadcast_multiply_fusion
  157.3 0.0 copy-done.1
  (4 shorter events, 0.1 us)
Async XLA Ops:
  7.2 120.0 %copy-start = (f32[32]{0:T(128)S(1)}, f32[32]{0:T(128)}, u32[]{:S(2)}) copy-start(f32[32]{0:T(128)} %param.14) | copy-start | bytes 388
  7.2 53.6 %copy-start.3 = (f32[1024]{0:T(1024)S(1)}, f32[1024]{0:T(1024)}, u32[]{:S(2)}) copy-start(f32[1024]{0:T(1024)} %param.9) | copy-start | bytes 12292
  7.2 51.0 %all-gather.2.cloned.1.call-start = ((), (), s32[]{:S(2)}) async-start(), calls=%async_computation.3 | async-start | bytes 2621440 | tf_op jit(solution)/shard_map/all_gather | solution.py:21
  18.2 54.9 %all-to-all-start = ((s32[4,1,1024]{2,1,0:T(1,128)}), s32[4,1,1024]{2,1,0:T(1,128)S(1)}, u32[]{:S(2)}, u32[]{:S(2)}) async-start(s32[4,1,1024]{2,1,0:T(1,128)} %bitcast.4), calls=%async_computation | async-start | bytes 32768 | tf_op jit(solution)/shard_map/all_to_all | solution.py:46
  22.4 124.3 %reduce-scatter.2.cloned.1.call-start = ((), (), s32[]{:S(2)}) async-start(), calls=%async_computation.4 | async-start | bytes 655360 | tf_op jit(solution)/shard_map/reduce_scatter | solution.py:54
  125.0 2.1 %copy-start.2 = (f32[4]{0:T(128)S(1)}, f32[4]{0:T(128)}, u32[]{:S(2)}) copy-start(f32[4]{0:T(128)} %param.15) | copy-start | bytes 52
  125.0 2.2 %copy-start.4 = (s32[256]{0:T(256)S(1)}, s32[256]{0:T(256)}, u32[]{:S(2)}) copy-start(s32[256]{0:T(256)} %param.13) | copy-start | bytes 3076
  147.7 9.5 %copy-start.1 = (f32[256,128]{1,0:T(8,128)}, f32[256,128]{1,0:T(8,128)S(1)}, u32[]{:S(2)}) copy-start(f32[256,128]{1,0:T(8,128)S(1)} %maximum_multiply_fusion) | copy-start | bytes 393220
Sparse Core Ops, SparseCore 0:
  9.6 48.5 all-gather.1
  127.2 19.4 reduce-scatter.1
where the time goes:
time: 165 us; the launch traced here: 164 us
  blocking collectives  60.6 us (37%)
  waiting for transfers between devices  55.8 us (34%)
  local copies, waits for them, and re-layouts  15.8 us (10%)
  between operations  14.2 us (9%)
  matrix products  6.79 us (4%)
  other arithmetic  6.63 us (4%)
  starting transfers between devices  4.28 us (3%)
    all_to_all x1, blocking collectives, shards(): lax.all_to_all(outgoing, 'owner', split_axis=0, concat_axis=0, tiled=True)  51.9 us
    all_gather x1, waiting for transfers between devices, shards(): shard_piece = lax.all_gather(shocks, 'path', axis=0, tiled=True)  35.8 us
    reduce_scatter x1, waiting for transfers between devices, shards(): lax.psum_scatter(partial_nets, 'path', scatter_dimension=1, tiled=True)  19.3 us
    unnamed x12, local copies, waits for them, and re-layouts  12.8 us
    psum x1, blocking collectives, shards(): path_totals = lax.psum(local_totals, 'path')  8.72 us
    dot_general x1, matrix products, shards(): lax.dot_general(sensitivity, flat_shocks, (((1,), (1,)), ((), ())), prefe...  4.55 us
    all_to_all x1, starting transfers between devices, shards(): lax.all_to_all(out_labels, 'owner', split_axis=0, concat_axis=0, tiled=True)  4.24 us
  transfers between devices with their start and end apart: 3, of which 2 were waited for; matrix products, arithmetic and copies ran while one was open for 15% of the time, Pallas kernels for 0%

commit v1 on v0

v1 whole, which is shorter than its diff:
```python
import functools

import jax
import jax.numpy as jnp
from jax import lax
from jax.experimental import pallas as pl
from jax.experimental.pallas import tpu as pltpu
from jax.sharding import PartitionSpec as P

MESH = pl.DeviceIdType.MESH
F32, BF16 = jnp.float32, jnp.bfloat16
BY_LANES = (((1,), (1,)), ((), ()))


def kernel(
    n_owner, n_path, n_sets, steps,
    sens_hbm, shock_ref, base_ref, key_ref, cset_ref, posted_ref, disc_ref,
    exp_ref, mean_ref,
    sens, moves, base_cols, hot, tv, send1, recv1, keep2, send2, recv2, acc, send3, recv3, tot, recv4,
    load_sem, a_send, a_recv, b_send, b_recv, c_send, c_recv,
    s1_send, s1_recv, s2_send, s2_recv, s3_send, s3_recv, s4_send, s4_recv,
):
    owner, me = lax.axis_index("owner"), lax.axis_index("path")
    n_y = n_owner // 2
    y, core = owner // 2, owner % 2
    partner = owner + 1 - 2 * core
    half = n_y * n_sets
    trades, factors = sens.shape
    cols = shock_ref.shape[0]
    piece = factors // n_owner
    open_sends = []

    def device(o, p):
        return {"owner": o, "path": p}

    def across(j):
        return lax.rem(y + j, n_y)

    def along(j):
        return lax.rem(me + j, n_path)

    load = pltpu.make_async_copy(sens_hbm, sens, load_sem)
    load.start()

    barrier = pltpu.get_barrier_semaphore()
    for j in range(1, n_path):
        pl.semaphore_signal(barrier, inc=1, device_id=device(owner, along(j)), device_id_type=MESH)
    for j in range(1, n_y):
        pl.semaphore_signal(
            barrier, inc=1, device_id=device(across(j) * 2 + core, me), device_id_type=MESH
        )
    pl.semaphore_signal(barrier, inc=1, device_id=device(partner, me), device_id_type=MESH)
    pl.semaphore_wait(barrier, n_path - 1 + n_y - 1 + 1)

    low_side = me <= n_path - 1 - me
    both = jnp.where(low_side, me, n_path - 1 - me)
    order = []
    for k in range(n_path):
        swing = me - (k + 1) // 2 if k % 2 else me + k // 2
        order.append(jnp.where(k <= 2 * both, swing, jnp.where(low_side, k, n_path - 1 - k)))

    def lanes(o):
        return pl.ds(pl.multiple_of(o * piece, piece), piece)

    def copy(src, dst, send_sem, recv_sem, target):
        return pltpu.make_async_remote_copy(
            src_ref=src, dst_ref=dst, send_sem=send_sem, recv_sem=recv_sem,
            device_id=target, device_id_type=MESH,
        )

    def go(c):
        c.start()
        open_sends.append(c)

    for k in range(1, n_path):
        go(copy(
            shock_ref.at[:, lanes(owner)], moves.at[me, :, lanes(owner)],
            a_send.at[k], a_recv.at[me], device(owner, order[k]),
        ))

    def spread(k):
        q = order[k]
        mine = moves.at[q, :, lanes(owner)]
        copy(mine, mine, a_send.at[k], a_recv.at[q], device(owner, q)).wait_recv()
        for j in range(1, n_y):
            go(copy(mine, mine, b_send.at[k, j], b_recv.at[q, j],
                    device(across(j) * 2 + core, me)))
        go(copy(mine, mine, c_send.at[k, 0], c_recv.at[q, 0], device(partner, me)))

    def relay(k):
        q = order[k]
        for j in range(1, n_y):
            source = across(n_y - j) * 2 + core
            got = moves.at[q, :, lanes(source)]
            copy(got, got, b_send.at[k, j], b_recv.at[q, j], device(partner, me)).wait_recv()
            go(copy(got, got, c_send.at[k, j], c_recv.at[q, j], device(partner, me)))

    def gathered(k):
        q = order[k]
        for j in range(n_y):
            got = moves.at[q, :, lanes(across(n_y - j) * 2 + 1 - core)]
            copy(got, got, c_send.at[k, j], c_recv.at[q, j], device(partner, me)).wait_recv()

    tile = min(trades, 512)

    def values(k):
        @pl.loop(0, trades // tile)
        def _(i):
            rows = pl.ds(pl.multiple_of(i * tile, tile), tile)
            block = shock_ref[...] if k == 0 else moves[order[k]]
            out = lax.dot_general(sens[rows, :], block, BY_LANES, preferred_element_type=F32)
            tv[k, rows, :] = (out + base_cols[rows, :]).astype(BF16)

        @pl.loop(0, n_y)
        def _(i):
            rows = pl.ds(pl.multiple_of(i * n_sets, n_sets), n_sets)
            send1[k, rows, :] = jnp.dot(hot[1, rows, :], tv[k], preferred_element_type=F32)

        go(copy(send1.at[k], recv1.at[k], s1_send.at[k], s1_recv.at[k], device(partner, me)))

    def set_sums(k, yy):
        rows = pl.ds(pl.multiple_of(yy * n_sets, n_sets), n_sets)
        return jnp.dot(hot[0, rows, :], tv[k], preferred_element_type=F32) + recv1[k, rows, :]

    def cross_owner(k):
        copy(send1.at[k], recv1.at[k], s1_send.at[k], s1_recv.at[k], device(partner, me)).wait_recv()
        for j in range(1, n_y):
            send2[k, j - 1] = set_sums(k, across(j)).astype(BF16)
            go(copy(send2.at[k, j - 1], recv2.at[k, j - 1], s2_send.at[k, j - 1],
                    s2_recv.at[k, j - 1], device(across(j) * 2 + core, me)))
        keep2[k] = set_sums(k, y)

    def cross_path(k):
        total = keep2[k]
        for j in range(1, n_y):
            copy(send2.at[k, j - 1], recv2.at[k, j - 1], s2_send.at[k, j - 1],
                 s2_recv.at[k, j - 1], device(partner, me)).wait_recv()
            total = total + recv2[k, j - 1].astype(F32)
        if k == 0:
            acc[...] = total
        else:
            send3[k - 1] = total.astype(BF16)
            go(copy(send3.at[k - 1], recv3.at[me], s3_send.at[k], s3_recv.at[me],
                    device(owner, order[k])))

    base_cols[...] = jnp.broadcast_to(base_ref[...], (cols, trades)).T
    for h in range(2):
        shift = jnp.where(core == h, 0, half)
        key = key_ref[...] - shift

        @pl.loop(0, n_y)
        def _(i):
            row = lax.broadcasted_iota(jnp.int32, (n_sets, trades), 0) + i * n_sets
            hot[h, pl.ds(pl.multiple_of(i * n_sets, n_sets), n_sets), :] = jnp.where(
                row == key, 1.0, 0.0
            ).astype(BF16)

    load.wait()

    for k in range(n_path + 2):
        if k + 1 < n_path:
            if k == 0:
                values(0)
                spread(1)
            relay(k + 1)
            if k + 2 < n_path:
                spread(k + 2)
        if 1 <= k < n_path:
            gathered(k)
            values(k)
        if 1 <= k < n_path + 1:
            cross_owner(k - 1)
        if k >= 2:
            cross_path(k - 2)

    floor = jnp.zeros((1, n_sets), F32)
    for a in range(posted_ref.shape[0]):
        floor = jnp.where(cset_ref[...] == a, posted_ref[a], floor)
    floor_cols = jnp.broadcast_to(floor, (cols, n_sets)).T
    lane_step = lax.broadcasted_iota(jnp.int32, (1, cols), 1) % steps
    factor = jnp.zeros((1, cols), F32)
    for s in range(steps):
        factor = jnp.where(lane_step == s, disc_ref[s], factor)
    nets = acc[...]
    for j in range(1, n_path):
        p = along(j)
        got = recv3.at[p]
        copy(got, got, s3_send.at[j], s3_recv.at[p], device(owner, p)).wait_recv()
        nets = nets + recv3[p].astype(F32)
    exposure = factor * jnp.maximum(nets - floor_cols, 0.0)
    exp_ref[...] = exposure

    pick = (
        lax.broadcasted_iota(jnp.int32, (8, cols), 1) % steps
        == lax.broadcasted_iota(jnp.int32, (8, cols), 0)
    ).astype(F32)
    tot[...] = lax.dot_general(
        pick, exposure, BY_LANES, precision=lax.Precision.HIGHEST, preferred_element_type=F32
    )
    for j in range(1, n_path):
        go(copy(tot, recv4.at[me], s4_send.at[j], s4_recv.at[me], device(owner, along(j))))
    sums = tot[...]
    for j in range(1, n_path):
        p = along(j)
        copy(tot, recv4.at[p], s4_send.at[j], s4_recv.at[p], device(owner, p)).wait_recv()
        sums = sums + recv4[p]
    mean_ref[...] = (sums / (cols // steps * n_path)).T[:, :steps]
    for c in open_sends:
        c.wait_send()


def shards(
    sensitivity,
    present_trade_value,
    trade_set_owner,
    trade_local_set,
    shocks,
    collateral_of_set,
    collateral_posted,
    discount,
):
    n_owner, n_path = lax.axis_size("owner"), lax.axis_size("path")
    trades, factors = sensitivity.shape
    steps = shocks.shape[1]
    cols = shocks.shape[0] * steps
    n_sets = collateral_of_set.shape[0]
    n_y = n_owner // 2
    half = n_y * n_sets
    owner_of = trade_set_owner[:, 0]
    key = (owner_of % 2) * half + (owner_of // 2) * n_sets + trade_local_set
    others = max(n_y - 1, 1)
    vmem = pl.BlockSpec(memory_space=pltpu.VMEM)
    smem = pl.BlockSpec(memory_space=pltpu.SMEM)
    dma = pltpu.SemaphoreType.DMA
    return pl.pallas_call(
        functools.partial(kernel, n_owner, n_path, n_sets, steps),
        out_shape=(
            jax.ShapeDtypeStruct((n_sets, cols), F32),
            jax.ShapeDtypeStruct((n_sets, steps), F32),
        ),
        in_specs=[pl.BlockSpec(memory_space=pl.ANY), vmem, vmem, vmem, vmem, smem, smem],
        out_specs=(vmem, vmem),
        scratch_shapes=[
            pltpu.VMEM((trades, factors), BF16),
            pltpu.VMEM((n_path, cols, factors), BF16),
            pltpu.VMEM((trades, cols), F32),
            pltpu.VMEM((2, half, trades), BF16),
            pltpu.VMEM((n_path, trades, cols), BF16),
            pltpu.VMEM((n_path, half, cols), F32),
            pltpu.VMEM((n_path, half, cols), F32),
            pltpu.VMEM((n_path, n_sets, cols), F32),
            pltpu.VMEM((n_path, others, n_sets, cols), BF16),
            pltpu.VMEM((n_path, others, n_sets, cols), BF16),
            pltpu.VMEM((n_sets, cols), F32),
            pltpu.VMEM((n_path - 1, n_sets, cols), BF16),
            pltpu.VMEM((n_path, n_sets, cols), BF16),
            pltpu.VMEM((8, n_sets), F32),
            pltpu.VMEM((n_path, 8, n_sets), F32),
            dma,
            dma((n_path,)), dma((n_path,)),
            dma((n_path, n_y)), dma((n_path, n_y)),
            dma((n_path, n_y)), dma((n_path, n_y)),
            dma((n_path,)), dma((n_path,)),
            dma((n_path, others)), dma((n_path, others)),
            dma((n_path,)), dma((n_path,)),
            dma((n_path,)), dma((n_path,)),
        ],
        compiler_params=pltpu.CompilerParams(
            collective_id=0, has_side_effects=True, vmem_limit_bytes=60 * 1024 * 1024
        ),
        cost_estimate=pl.CostEstimate(
            flops=2 * trades * cols * n_path * (factors + 2 * half),
            bytes_accessed=2 * trades * factors,
            transcendentals=0,
        ),
    )(
        sensitivity,
        shocks.reshape(cols, factors),
        present_trade_value.reshape(1, trades),
        key.reshape(1, trades),
        collateral_of_set.reshape(1, n_sets),
        collateral_posted,
        discount,
    )


def solution(mesh):
    in_specs = (
        P(("groups", "owner", "path"), None),
        P(("groups", "owner", "path")),
        P(("groups", "owner", "path"), None),
        P(("groups", "owner", "path")),
        P(("groups", "path"), None, None),
        P(("groups", "owner")),
        P("groups"),
        P("groups"),
    )
    out_specs = (P(("groups", "owner"), "path"), P(("groups", "owner"), None))
    return jax.shard_map(shards, mesh=mesh, in_specs=in_specs, out_specs=out_specs, check_vma=False)
```

time: 165 us -> 54.8 us (0.33)
  blocking collectives: 60.6 us -> 0 us
  waiting for transfers between devices: 55.8 us -> 0 us
  Pallas kernels: 0 us -> 47.5 us
  between operations: 14.2 us -> 0.64 us
  local copies, waits for them, and re-layouts: 15.8 us -> 5.09 us
  matrix products: 6.79 us -> 0 us
  other arithmetic: 6.63 us -> 1.31 us
  starting transfers between devices: 4.28 us -> 0 us
    all_to_all x1 -> x0, blocking collectives: 51.9 us -> none  [shards(): lax.all_to_all(outgoing, 'owner', split_axis=0, concat_axis=0, tiled=True)]
    pallas_call x0 -> x1, Pallas kernels: none -> 47.5 us  [shards(): pl.pallas_call(functools.partial(kernel, n_owner, n_path, n_sets, steps),...]
    all_gather x1 -> x0, waiting for transfers between devices: 35.8 us -> none  [shards(): shard_piece = lax.all_gather(shocks, 'path', axis=0, tiled=True)]
    reduce_scatter x1 -> x0, waiting for transfers between devices: 19.3 us -> none  [shards(): lax.psum_scatter(partial_nets, 'path', scatter_dimension=1, tiled=True)]
    unnamed x12 -> x1, local copies, waits for them, and re-layouts: 12.8 us -> 1.57 us
    psum x1 -> x0, blocking collectives: 8.72 us -> none  [shards(): path_totals = lax.psum(local_totals, 'path')]
    dot_general x3 -> x0, matrix products: 6.79 us -> none  [the longest x1 4.55 us: shards(): lax.dot_general(sensitivity, flat_shocks, (((1,), (1,)), ((), ())), prefe...]
    all_to_all x1 -> x0, starting transfers between devices: 4.24 us -> none  [shards(): lax.all_to_all(out_labels, 'owner', split_axis=0, concat_axis=0, tiled=True)]
  transfers between devices with their start and end apart: 3 -> 0, of which waited for: 2 -> 0; matrix products, arithmetic and copies ran while one was open for 15% -> 0% of each run, Pallas kernels for 0% -> 0%
where the time goes in v1:
time: 54.8 us; the launch traced here: 54.5 us
  Pallas kernels  47.5 us (87%)
  local copies, waits for them, and re-layouts  5.09 us (9%)
  other arithmetic  1.31 us (2%)
  between operations  0.64 us (1%)
    pallas_call x1, Pallas kernels, shards(): pl.pallas_call(functools.partial(kernel, n_owner, n_path, n_sets, steps),...  47.5 us
    reshape x1, local copies, waits for them, and re-layouts, shards(): shocks.reshape(cols, factors)  1.94 us
    pallas_call x1, local copies, waits for them, and re-layouts, shards(): pl.pallas_call(functools.partial(kernel, n_owner, n_path, n_sets, steps),...  1.58 us
    unnamed x1, local copies, waits for them, and re-layouts  1.57 us
    add x1, other arithmetic, shards(): key = owner_of % 2 * half + owner_of // 2 * n_sets + trade_local_set  1.31 us

profile of v1, /device:TPU:0, one launch (start us, length us, event | category | flops | bytes accessed | tf_op | source)
XLA Modules:
  0.0 54.5 jit_solution(12150367911731755426)
XLA Ops:
  0.6 1.3 %fusion.2 = s32[1024]{0:T(1024)} fusion(s32[1024]{0:T(1024)} %param.11, s32[1024]{0:T(1024)} %bitcast.4), kind=kLoop, calls=%fused_computation.7 | loop fusion | flops 23552 | bytes 12288 | tf_op jit(solution)/shard_map/add | solution.py:230
  1.9 1.9 %reshape.16.shock_ref = bf16[128,2048]{1,0:T(8,128)(2,1)} reshape(bf16[32,4,2048]{2,1,0:T(4,128)(2,1)} %param.12) | data formatting | bytes 1048576 | tf_op jit(solution)/shard_map/reshape | solution.py:278
  3.9 47.5 %shard_map.95 = (f32[256,128]{1,0:T(8,128)}, f32[256,4]{1,0:T(8,128)}) custom-call(bf16[1024,2048]{1,0:T(8,128)(2,1)} %sens_hbm.1, bf16[128,2048]{1,0:T(8,128)(2,1)} %reshape.16.shock_ref, f32[1,1024]{1,0:T(1,128)} %bitcast.6, s32[1,1024]{1,0:T(1,128)} %bitcast.5, s32[1,256]{1,0:T(1,128)} %bitcast.7, f32[32]{0:T(128)} %posted_ref.1, f32[4]{0:T(128)} %disc_ref.1), custom_call_target="tpu_custom_call" | custom-call | flops 3221225472 | bytes 4194304 | tf_op jit(solution)/shard_map/pallas_call | solution.py:235
  51.4 1.6 %copy.10 = f32[256,4]{0,1:T(4,128)} copy(f32[256,4]{1,0:T(8,128)} %get-tuple-element.3) | data formatting | bytes 8192 | tf_op jit(solution)/shard_map/pallas_call | solution.py:235
  52.9 1.6 %copy.12 = f32[256,128]{1,0:T(8,128)} copy(f32[256,128]{1,0:T(8,128)} %get-tuple-element.6) | data formatting | bytes 262144

commit v2 on v1

--- a/solution.py
+++ b/solution.py
@@ -14,7 +14,7 @@
 
 def kernel(
     n_owner, n_path, n_sets, steps,
-    sens_hbm, shock_ref, base_ref, key_ref, cset_ref, posted_ref, disc_ref,
+    sens_hbm, shock_ref, base_ref, owner_ref, local_ref, cset_ref, posted_ref, disc_ref,
     exp_ref, mean_ref,
     sens, moves, base_cols, hot, tv, send1, recv1, keep2, send2, recv2, acc, send3, recv3, tot, recv4,
     load_sem, a_send, a_recv, b_send, b_recv, c_send, c_recv,
@@ -28,7 +28,7 @@
     trades, factors = sens.shape
     cols = shock_ref.shape[0]
     piece = factors // n_owner
-    open_sends = []
+    open_sends, edge_sends = [], []
 
     def device(o, p):
         return {"owner": o, "path": p}
@@ -50,6 +50,7 @@
             barrier, inc=1, device_id=device(across(j) * 2 + core, me), device_id_type=MESH
         )
     pl.semaphore_signal(barrier, inc=1, device_id=device(partner, me), device_id_type=MESH)
+    base_cols[...] = jnp.broadcast_to(base_ref[...], (cols, trades)).T
     pl.semaphore_wait(barrier, n_path - 1 + n_y - 1 + 1)
 
     low_side = me <= n_path - 1 - me
@@ -72,16 +73,25 @@
         c.start()
         open_sends.append(c)
 
-    for k in range(1, n_path):
-        go(copy(
-            shock_ref.at[:, lanes(owner)], moves.at[me, :, lanes(owner)],
-            a_send.at[k], a_recv.at[me], device(owner, order[k]),
-        ))
+    def hop(src, target, slot, q):
+        inside = (target >= 0) & (target < n_path)
+        c = copy(src, moves.at[q, :, lanes(owner)], a_send.at[slot], a_recv.at[q],
+                 device(owner, jnp.clip(target, 0, n_path - 1)))
+
+        @pl.when(inside)
+        def _():
+            c.start()
+
+        edge_sends.append((inside, c))
+
+    hop(shock_ref.at[:, lanes(owner)], me + 1, 0, me)
+    hop(shock_ref.at[:, lanes(owner)], me - 1, n_path, me)
 
     def spread(k):
         q = order[k]
         mine = moves.at[q, :, lanes(owner)]
         copy(mine, mine, a_send.at[k], a_recv.at[q], device(owner, q)).wait_recv()
+        hop(mine, jnp.where(q < me, me + 1, me - 1), k, q)
         for j in range(1, n_y):
             go(copy(mine, mine, b_send.at[k, j], b_recv.at[q, j],
                     device(across(j) * 2 + core, me)))
@@ -143,10 +153,9 @@
             go(copy(send3.at[k - 1], recv3.at[me], s3_send.at[k], s3_recv.at[me],
                     device(owner, order[k])))
 
-    base_cols[...] = jnp.broadcast_to(base_ref[...], (cols, trades)).T
-    for h in range(2):
-        shift = jnp.where(core == h, 0, half)
-        key = key_ref[...] - shift
+    place = (owner_ref[...] % 2) * half + (owner_ref[...] // 2) * n_sets + local_ref[...]
+    def one_hots(h):
+        key = place - jnp.where(core == h, 0, half)
 
         @pl.loop(0, n_y)
         def _(i):
@@ -155,20 +164,25 @@
                 row == key, 1.0, 0.0
             ).astype(BF16)
 
+    one_hots(1)
+    spread(1)
+    one_hots(0)
+    if n_path > 2:
+        spread(2)
     load.wait()
-
-    for k in range(n_path + 2):
-        if k + 1 < n_path:
-            if k == 0:
-                values(0)
-                spread(1)
-            relay(k + 1)
-            if k + 2 < n_path:
-                spread(k + 2)
-        if 1 <= k < n_path:
+    values(0)
+    relay(1)
+    for k in range(1, n_path + 2):
+        if k + 2 < n_path:
+            spread(k + 2)
+        if k == 1 and n_path > 2:
+            relay(2)
+        if k < n_path:
             gathered(k)
             values(k)
-        if 1 <= k < n_path + 1:
+        if 1 < k < n_path - 1:
+            relay(k + 1)
+        if k < n_path + 1:
             cross_owner(k - 1)
         if k >= 2:
             cross_path(k - 2)
@@ -204,9 +218,14 @@
         p = along(j)
         copy(tot, recv4.at[p], s4_send.at[j], s4_recv.at[p], device(owner, p)).wait_recv()
         sums = sums + recv4[p]
-    mean_ref[...] = (sums / (cols // steps * n_path)).T[:, :steps]
+    mean_ref[...] = (sums / (cols // steps * n_path))[:steps, :]
     for c in open_sends:
         c.wait_send()
+    for inside, c in edge_sends:
+
+        @pl.when(inside)
+        def _():
+            c.wait_send()
 
 
 def shards(
@@ -226,19 +245,17 @@
     n_sets = collateral_of_set.shape[0]
     n_y = n_owner // 2
     half = n_y * n_sets
-    owner_of = trade_set_owner[:, 0]
-    key = (owner_of % 2) * half + (owner_of // 2) * n_sets + trade_local_set
     others = max(n_y - 1, 1)
     vmem = pl.BlockSpec(memory_space=pltpu.VMEM)
     smem = pl.BlockSpec(memory_space=pltpu.SMEM)
     dma = pltpu.SemaphoreType.DMA
-    return pl.pallas_call(
+    exposure, mean = pl.pallas_call(
         functools.partial(kernel, n_owner, n_path, n_sets, steps),
         out_shape=(
             jax.ShapeDtypeStruct((n_sets, cols), F32),
-            jax.ShapeDtypeStruct((n_sets, steps), F32),
+            jax.ShapeDtypeStruct((steps, n_sets), F32),
         ),
-        in_specs=[pl.BlockSpec(memory_space=pl.ANY), vmem, vmem, vmem, vmem, smem, smem],
+        in_specs=[pl.BlockSpec(memory_space=pl.ANY), vmem, vmem, vmem, vmem, vmem, smem, smem],
         out_specs=(vmem, vmem),
         scratch_shapes=[
             pltpu.VMEM((trades, factors), BF16),
@@ -257,7 +274,7 @@
             pltpu.VMEM((8, n_sets), F32),
             pltpu.VMEM((n_path, 8, n_sets), F32),
             dma,
-            dma((n_path,)), dma((n_path,)),
+            dma((n_path + 1,)), dma((n_path,)),
             dma((n_path, n_y)), dma((n_path, n_y)),
             dma((n_path, n_y)), dma((n_path, n_y)),
             dma((n_path,)), dma((n_path,)),
@@ -277,11 +294,13 @@
         sensitivity,
         shocks.reshape(cols, factors),
         present_trade_value.reshape(1, trades),
-        key.reshape(1, trades),
+        trade_set_owner.reshape(1, trades),
+        trade_local_set.reshape(1, trades),
         collateral_of_set.reshape(1, n_sets),
         collateral_posted,
         discount,
     )
+    return exposure, mean.T
 
 
 def solution(mesh):

time: 54.8 us -> 49.3 us (0.90)
  Pallas kernels: 47.5 us -> 43.6 us
  other arithmetic: 1.31 us -> 0 us
    pallas_call x1, Pallas kernels: 47.5 us -> 43.6 us  [shards(): pl.pallas_call(functools.partial(kernel, n_owner, n_path, n_sets, steps),...]
    pallas_call x1 -> x0, local copies, waits for them, and re-layouts: 1.58 us -> none  [shards(): pl.pallas_call(functools.partial(kernel, n_owner, n_path, n_sets, steps),...]
    add x1 -> x0, other arithmetic: 1.31 us -> none  [shards(): key = owner_of % 2 * half + owner_of // 2 * n_sets + trade_local_set]
    unnamed x1 -> x2, local copies, waits for them, and re-layouts: 1.57 us -> 2.84 us
where the time goes in v2:
time: 49.3 us; the launch traced here: 49.1 us
  Pallas kernels  43.6 us (88%)
  local copies, waits for them, and re-layouts  4.79 us (10%)
  between operations  0.64 us (1%)
    pallas_call x1, Pallas kernels, shards(): pl.pallas_call(functools.partial(kernel, n_owner, n_path, n_sets, steps),...  43.6 us
    unnamed x2, local copies, waits for them, and re-layouts  2.84 us
    reshape x1, local copies, waits for them, and re-layouts, shards(): shocks.reshape(cols, factors)  1.94 us

profile of v2, /device:TPU:0, one launch (start us, length us, event | category | flops | bytes accessed | tf_op | source)
XLA Modules:
  0.0 49.1 jit_solution(6746740661891664185)
XLA Ops:
  0.6 1.9 %reshape.19.shock_ref = bf16[128,2048]{1,0:T(8,128)(2,1)} reshape(bf16[32,4,2048]{2,1,0:T(4,128)(2,1)} %param.12) | data formatting | bytes 1048576 | tf_op jit(solution)/shard_map/reshape | solution.py:295
  2.6 43.6 %shard_map.95 = (f32[256,128]{1,0:T(8,128)}, f32[4,256]{1,0:T(4,128)}) custom-call(bf16[1024,2048]{1,0:T(8,128)(2,1)} %sens_hbm.1, bf16[128,2048]{1,0:T(8,128)(2,1)} %reshape.19.shock_ref, f32[1,1024]{1,0:T(1,128)} %bitcast.6, s32[1,1024]{1,0:T(1,128)} %bitcast.7, s32[1,1024]{1,0:T(1,128)} %bitcast.8, s32[1,256]{1,0:T(1,128)} %bitcast.9, f32[32]{0:T(128)} %posted_ref.1, ...), custom_call_target="tpu_custom_call" | custom-call | flops 3221225472 | bytes 4194304 | tf_op jit(solution)/shard_map/pallas_call | solution.py:252
  46.2 1.6 %copy.12 = f32[256,128]{1,0:T(8,128)} copy(f32[256,128]{1,0:T(8,128)} %get-tuple-element.8) | data formatting | bytes 262144
  47.8 1.3 %copy.13 = f32[256,4]{0,1:T(4,128)} copy(f32[256,4]{0,1:T(4,128)} %bitcast.5) | data formatting | bytes 8192

commit v3 on v2

--- a/solution.py
+++ b/solution.py
@@ -9,14 +9,15 @@
 
 MESH = pl.DeviceIdType.MESH
 F32, BF16 = jnp.float32, jnp.bfloat16
+PARTS = 2
 BY_LANES = (((1,), (1,)), ((), ()))
 
 
 def kernel(
     n_owner, n_path, n_sets, steps,
-    sens_hbm, shock_ref, base_ref, owner_ref, local_ref, cset_ref, posted_ref, disc_ref,
+    sens_hbm, shock_block, base_ref, owner_ref, local_ref, cset_ref, posted_ref, disc_ref,
     exp_ref, mean_ref,
-    sens, moves, base_cols, hot, tv, send1, recv1, keep2, send2, recv2, acc, send3, recv3, tot, recv4,
+    shock_ref, sens, moves, base_cols, hot, tv, send1, recv1, keep2, send2, recv2, acc, send3, recv3, tot, recv4,
     load_sem, a_send, a_recv, b_send, b_recv, c_send, c_recv,
     s1_send, s1_recv, s2_send, s2_recv, s3_send, s3_recv, s4_send, s4_recv,
 ):
@@ -50,6 +51,7 @@
             barrier, inc=1, device_id=device(across(j) * 2 + core, me), device_id_type=MESH
         )
     pl.semaphore_signal(barrier, inc=1, device_id=device(partner, me), device_id_type=MESH)
+    shock_ref[...] = shock_block[...].reshape(cols, factors)
     base_cols[...] = jnp.broadcast_to(base_ref[...], (cols, trades)).T
     pl.semaphore_wait(barrier, n_path - 1 + n_y - 1 + 1)
 
@@ -73,10 +75,13 @@
         c.start()
         open_sends.append(c)
 
-    def hop(src, target, slot, q):
+    def rows_of(part):
+        return pl.ds(part * (cols // PARTS), cols // PARTS)
+
+    def hop(src, target, slot, q, part):
         inside = (target >= 0) & (target < n_path)
-        c = copy(src, moves.at[q, :, lanes(owner)], a_send.at[slot], a_recv.at[q],
-                 device(owner, jnp.clip(target, 0, n_path - 1)))
+        c = copy(src, moves.at[q, rows_of(part), lanes(owner)], a_send.at[slot, part],
+                 a_recv.at[q, part], device(owner, jnp.clip(target, 0, n_path - 1)))
 
         @pl.when(inside)
         def _():
@@ -84,32 +89,39 @@
 
         edge_sends.append((inside, c))
 
-    hop(shock_ref.at[:, lanes(owner)], me + 1, 0, me)
-    hop(shock_ref.at[:, lanes(owner)], me - 1, n_path, me)
+    for part in range(PARTS):
+        hop(shock_ref.at[rows_of(part), lanes(owner)], me + 1, 0, me, part)
+        hop(shock_ref.at[rows_of(part), lanes(owner)], me - 1, n_path, me, part)
 
     def spread(k):
         q = order[k]
-        mine = moves.at[q, :, lanes(owner)]
-        copy(mine, mine, a_send.at[k], a_recv.at[q], device(owner, q)).wait_recv()
-        hop(mine, jnp.where(q < me, me + 1, me - 1), k, q)
-        for j in range(1, n_y):
-            go(copy(mine, mine, b_send.at[k, j], b_recv.at[q, j],
-                    device(across(j) * 2 + core, me)))
-        go(copy(mine, mine, c_send.at[k, 0], c_recv.at[q, 0], device(partner, me)))
+        for part in range(PARTS):
+            mine = moves.at[q, rows_of(part), lanes(owner)]
+            copy(mine, mine, a_send.at[k, part], a_recv.at[q, part], device(owner, q)).wait_recv()
+            hop(mine, jnp.where(q < me, me + 1, me - 1), k, q, part)
+            for j in range(1, n_y):
+                go(copy(mine, mine, b_send.at[k, j, part], b_recv.at[q, j, part],
+                        device(across(j) * 2 + core, me)))
+            go(copy(mine, mine, c_send.at[k, 0, part], c_recv.at[q, 0, part], device(partner, me)))
 
     def relay(k):
         q = order[k]
-        for j in range(1, n_y):
-            source = across(n_y - j) * 2 + core
-            got = moves.at[q, :, lanes(source)]
-            copy(got, got, b_send.at[k, j], b_recv.at[q, j], device(partner, me)).wait_recv()
-            go(copy(got, got, c_send.at[k, j], c_recv.at[q, j], device(partner, me)))
+        for part in range(PARTS):
+            for j in range(1, n_y):
+                source = across(n_y - j) * 2 + core
+                got = moves.at[q, rows_of(part), lanes(source)]
+                copy(got, got, b_send.at[k, j, part], b_recv.at[q, j, part],
+                     device(partner, me)).wait_recv()
+                go(copy(got, got, c_send.at[k, j, part], c_recv.at[q, j, part],
+                        device(partner, me)))
 
     def gathered(k):
         q = order[k]
-        for j in range(n_y):
-            got = moves.at[q, :, lanes(across(n_y - j) * 2 + 1 - core)]
-            copy(got, got, c_send.at[k, j], c_recv.at[q, j], device(partner, me)).wait_recv()
+        for part in range(PARTS):
+            for j in range(n_y):
+                got = moves.at[q, rows_of(part), lanes(across(n_y - j) * 2 + 1 - core)]
+                copy(got, got, c_send.at[k, j, part], c_recv.at[q, j, part],
+                     device(partner, me)).wait_recv()
 
     tile = min(trades, 512)
 
@@ -258,6 +270,7 @@
         in_specs=[pl.BlockSpec(memory_space=pl.ANY), vmem, vmem, vmem, vmem, vmem, smem, smem],
         out_specs=(vmem, vmem),
         scratch_shapes=[
+            pltpu.VMEM((cols, factors), BF16),
             pltpu.VMEM((trades, factors), BF16),
             pltpu.VMEM((n_path, cols, factors), BF16),
             pltpu.VMEM((trades, cols), F32),
@@ -274,9 +287,9 @@
             pltpu.VMEM((8, n_sets), F32),
             pltpu.VMEM((n_path, 8, n_sets), F32),
             dma,
-            dma((n_path + 1,)), dma((n_path,)),
-            dma((n_path, n_y)), dma((n_path, n_y)),
-            dma((n_path, n_y)), dma((n_path, n_y)),
+            dma((n_path + 1, PARTS)), dma((n_path, PARTS)),
+            dma((n_path, n_y, PARTS)), dma((n_path, n_y, PARTS)),
+            dma((n_path, n_y, PARTS)), dma((n_path, n_y, PARTS)),
             dma((n_path,)), dma((n_path,)),
             dma((n_path, others)), dma((n_path, others)),
             dma((n_path,)), dma((n_path,)),
@@ -292,7 +305,7 @@
         ),
     )(
         sensitivity,
-        shocks.reshape(cols, factors),
+        shocks,
         present_trade_value.reshape(1, trades),
         trade_set_owner.reshape(1, trades),
         trade_local_set.reshape(1, trades),

time: 49.3 us -> 47 us (0.953)
  local copies, waits for them, and re-layouts: 4.79 us -> 2.85 us
    reshape x1 -> x0, local copies, waits for them, and re-layouts: 1.94 us -> none  [shards(): shocks.reshape(cols, factors)]
where the time goes in v3:
time: 47 us; the launch traced here: 46.9 us
  Pallas kernels  43.4 us (92%)
  local copies, waits for them, and re-layouts  2.85 us (6%)
  between operations  0.64 us (1%)
    pallas_call x1, Pallas kernels, shards(): pl.pallas_call(functools.partial(kernel, n_owner, n_path, n_sets, steps),...  43.4 us
    unnamed x2, local copies, waits for them, and re-layouts  2.85 us

profile of v3, /device:TPU:0, one launch (start us, length us, event | category | flops | bytes accessed | tf_op | source)
XLA Modules:
  0.0 46.9 jit_solution(8680865710290962266)
XLA Ops:
  0.6 43.4 %shard_map.95 = (f32[256,128]{1,0:T(8,128)}, f32[4,256]{1,0:T(4,128)}) custom-call(bf16[1024,2048]{1,0:T(8,128)(2,1)} %sens_hbm.1, bf16[32,4,2048]{2,1,0:T(4,128)(2,1)} %shock_block.1, f32[1,1024]{1,0:T(1,128)} %bitcast.6, s32[1,1024]{1,0:T(1,128)} %bitcast.7, s32[1,1024]{1,0:T(1,128)} %bitcast.8, s32[1,256]{1,0:T(1,128)} %bitcast.9, f32[32]{0:T(128)} %posted_ref.1, ...), custom_call_target="tpu_custom_call" | custom-call | flops 3221225472 | bytes 4194304 | tf_op jit(solution)/shard_map/pallas_call | solution.py:264
  44.0 1.6 %copy.12 = f32[256,128]{1,0:T(8,128)} copy(f32[256,128]{1,0:T(8,128)} %get-tuple-element.8) | data formatting | bytes 262144
  45.6 1.3 %copy.13 = f32[256,4]{0,1:T(4,128)} copy(f32[256,4]{0,1:T(4,128)} %bitcast.5) | data formatting | bytes 8192

commit v4 on v3

--- a/solution.py
+++ b/solution.py
@@ -136,13 +136,14 @@
         @pl.loop(0, n_y)
         def _(i):
             rows = pl.ds(pl.multiple_of(i * n_sets, n_sets), n_sets)
-            send1[k, rows, :] = jnp.dot(hot[1, rows, :], tv[k], preferred_element_type=F32)
+            part_sums = jnp.dot(hot[1, rows, :], tv[k], preferred_element_type=F32)
+            send1[k, rows, :] = part_sums.astype(BF16)
 
         go(copy(send1.at[k], recv1.at[k], s1_send.at[k], s1_recv.at[k], device(partner, me)))
 
     def set_sums(k, yy):
         rows = pl.ds(pl.multiple_of(yy * n_sets, n_sets), n_sets)
-        return jnp.dot(hot[0, rows, :], tv[k], preferred_element_type=F32) + recv1[k, rows, :]
+        return jnp.dot(hot[0, rows, :], tv[k], preferred_element_type=F32) + recv1[k, rows, :].astype(F32)
 
     def cross_owner(k):
         copy(send1.at[k], recv1.at[k], s1_send.at[k], s1_recv.at[k], device(partner, me)).wait_recv()
@@ -276,8 +277,8 @@
             pltpu.VMEM((trades, cols), F32),
             pltpu.VMEM((2, half, trades), BF16),
             pltpu.VMEM((n_path, trades, cols), BF16),
-            pltpu.VMEM((n_path, half, cols), F32),
-            pltpu.VMEM((n_path, half, cols), F32),
+            pltpu.VMEM((n_path, half, cols), BF16),
+            pltpu.VMEM((n_path, half, cols), BF16),
             pltpu.VMEM((n_path, n_sets, cols), F32),
             pltpu.VMEM((n_path, others, n_sets, cols), BF16),
             pltpu.VMEM((n_path, others, n_sets, cols), BF16),

time: 47 us -> 46.9 us (level)
  no operation moved by 1% of the time
where the time goes in v4:
time: 46.9 us; the launch traced here: 46.7 us
  Pallas kernels  43.2 us (92%)
  local copies, waits for them, and re-layouts  2.85 us (6%)
  between operations  0.64 us (1%)
    pallas_call x1, Pallas kernels, shards(): pl.pallas_call(functools.partial(kernel, n_owner, n_path, n_sets, steps),...  43.2 us
    unnamed x2, local copies, waits for them, and re-layouts  2.85 us

profile of v4, /device:TPU:0, one launch (start us, length us, event | category | flops | bytes accessed | tf_op | source)
XLA Modules:
  0.0 46.7 jit_solution(14108373479953444700)
XLA Ops:
  0.6 43.2 %shard_map.95 = (f32[256,128]{1,0:T(8,128)}, f32[4,256]{1,0:T(4,128)}) custom-call(bf16[1024,2048]{1,0:T(8,128)(2,1)} %sens_hbm.1, bf16[32,4,2048]{2,1,0:T(4,128)(2,1)} %shock_block.1, f32[1,1024]{1,0:T(1,128)} %bitcast.6, s32[1,1024]{1,0:T(1,128)} %bitcast.7, s32[1,1024]{1,0:T(1,128)} %bitcast.8, s32[1,256]{1,0:T(1,128)} %bitcast.9, f32[32]{0:T(128)} %posted_ref.1, ...), custom_call_target="tpu_custom_call" | custom-call | flops 3221225472 | bytes 4194304 | tf_op jit(solution)/shard_map/pallas_call | solution.py:265
  43.8 1.6 %copy.12 = f32[256,128]{1,0:T(8,128)} copy(f32[256,128]{1,0:T(8,128)} %get-tuple-element.8) | data formatting | bytes 262144
  45.4 1.3 %copy.13 = f32[256,4]{0,1:T(4,128)} copy(f32[256,4]{0,1:T(4,128)} %bitcast.5) | data formatting | bytes 8192

commit v5 on v4

--- a/solution.py
+++ b/solution.py
@@ -17,7 +17,7 @@
     n_owner, n_path, n_sets, steps,
     sens_hbm, shock_block, base_ref, owner_ref, local_ref, cset_ref, posted_ref, disc_ref,
     exp_ref, mean_ref,
-    shock_ref, sens, moves, base_cols, hot, tv, send1, recv1, keep2, send2, recv2, acc, send3, recv3, tot, recv4,
+    shock_ref, sens, moves, base_cols, floor_cols, hot, tv, send1, recv1, keep2, send2, recv2, acc, send3, recv3, tot, recv4,
     load_sem, a_send, a_recv, b_send, b_recv, c_send, c_recv,
     s1_send, s1_recv, s2_send, s2_recv, s3_send, s3_recv, s4_send, s4_recv,
 ):
@@ -52,7 +52,6 @@
         )
     pl.semaphore_signal(barrier, inc=1, device_id=device(partner, me), device_id_type=MESH)
     shock_ref[...] = shock_block[...].reshape(cols, factors)
-    base_cols[...] = jnp.broadcast_to(base_ref[...], (cols, trades)).T
     pl.semaphore_wait(barrier, n_path - 1 + n_y - 1 + 1)
 
     low_side = me <= n_path - 1 - me
@@ -123,7 +122,7 @@
                 copy(got, got, c_send.at[k, j, part], c_recv.at[q, j, part],
                      device(partner, me)).wait_recv()
 
-    tile = min(trades, 512)
+    tile = trades
 
     def values(k):
         @pl.loop(0, trades // tile)
@@ -177,11 +176,16 @@
                 row == key, 1.0, 0.0
             ).astype(BF16)
 
+    base_cols[...] = jnp.broadcast_to(base_ref[...], (cols, trades)).T
+    spread(1)
     one_hots(1)
-    spread(1)
     one_hots(0)
     if n_path > 2:
         spread(2)
+    floor = jnp.zeros((1, n_sets), F32)
+    for a in range(posted_ref.shape[0]):
+        floor = jnp.where(cset_ref[...] == a, posted_ref[a], floor)
+    floor_cols[...] = jnp.broadcast_to(floor, (cols, n_sets)).T
     load.wait()
     values(0)
     relay(1)
@@ -200,10 +204,6 @@
         if k >= 2:
             cross_path(k - 2)
 
-    floor = jnp.zeros((1, n_sets), F32)
-    for a in range(posted_ref.shape[0]):
-        floor = jnp.where(cset_ref[...] == a, posted_ref[a], floor)
-    floor_cols = jnp.broadcast_to(floor, (cols, n_sets)).T
     lane_step = lax.broadcasted_iota(jnp.int32, (1, cols), 1) % steps
     factor = jnp.zeros((1, cols), F32)
     for s in range(steps):
@@ -214,8 +214,7 @@
         got = recv3.at[p]
         copy(got, got, s3_send.at[j], s3_recv.at[p], device(owner, p)).wait_recv()
         nets = nets + recv3[p].astype(F32)
-    exposure = factor * jnp.maximum(nets - floor_cols, 0.0)
-    exp_ref[...] = exposure
+    exposure = factor * jnp.maximum(nets - floor_cols[...], 0.0)
 
     pick = (
         lax.broadcasted_iota(jnp.int32, (8, cols), 1) % steps
@@ -226,6 +225,7 @@
     )
     for j in range(1, n_path):
         go(copy(tot, recv4.at[me], s4_send.at[j], s4_recv.at[me], device(owner, along(j))))
+    exp_ref[...] = exposure
     sums = tot[...]
     for j in range(1, n_path):
         p = along(j)
@@ -275,6 +275,7 @@
             pltpu.VMEM((trades, factors), BF16),
             pltpu.VMEM((n_path, cols, factors), BF16),
             pltpu.VMEM((trades, cols), F32),
+            pltpu.VMEM((n_sets, cols), F32),
             pltpu.VMEM((2, half, trades), BF16),
             pltpu.VMEM((n_path, trades, cols), BF16),
             pltpu.VMEM((n_path, half, cols), BF16),

time: 46.9 us -> 46.5 us (level)
  no operation moved by 1% of the time
where the time goes in v5:
time: 46.5 us; the launch traced here: 46.3 us
  Pallas kernels  42.8 us (92%)
  local copies, waits for them, and re-layouts  2.85 us (6%)
  between operations  0.64 us (1%)
    pallas_call x1, Pallas kernels, shards(): pl.pallas_call(functools.partial(kernel, n_owner, n_path, n_sets, steps),...  42.8 us
    unnamed x2, local copies, waits for them, and re-layouts  2.85 us

profile of v5, /device:TPU:0, one launch (start us, length us, event | category | flops | bytes accessed | tf_op | source)
XLA Modules:
  0.0 46.3 jit_solution(4873235660128538708)
XLA Ops:
  0.6 42.8 %shard_map.95 = (f32[256,128]{1,0:T(8,128)}, f32[4,256]{1,0:T(4,128)}) custom-call(bf16[1024,2048]{1,0:T(8,128)(2,1)} %sens_hbm.1, bf16[32,4,2048]{2,1,0:T(4,128)(2,1)} %shock_block.1, f32[1,1024]{1,0:T(1,128)} %bitcast.6, s32[1,1024]{1,0:T(1,128)} %bitcast.7, s32[1,1024]{1,0:T(1,128)} %bitcast.8, s32[1,256]{1,0:T(1,128)} %bitcast.9, f32[32]{0:T(128)} %posted_ref.1, ...), custom_call_target="tpu_custom_call" | custom-call | flops 3221225472 | bytes 4194304 | tf_op jit(solution)/shard_map/pallas_call | solution.py:265
  43.5 1.6 %copy.12 = f32[256,128]{1,0:T(8,128)} copy(f32[256,128]{1,0:T(8,128)} %get-tuple-element.8) | data formatting | bytes 262144
  45.1 1.3 %copy.13 = f32[256,4]{0,1:T(4,128)} copy(f32[256,4]{0,1:T(4,128)} %bitcast.5) | data formatting | bytes 8192
